TPU v7x, 32 devices: a whole 2x2x4 slice. The times are simulated.
32 devices in a mesh: blk: 8 (over y, x, core), grp: 4 (over z).
Axes of the slice: x: 2, y: 2, z: 4, core: 2. Of those that a mesh axis runs over, the one named last changes fastest.
Arguments:
- user_factors: float32 [32768, 128], P(('blk', 'grp')), may hold values from -1.8 to 1.8
- user_accum: float32 [32768], P(('blk', 'grp')), may hold values from 10 to 200
- friend_factors: float32 [32768, 128], P(('blk', 'grp')), may hold values from -1.8 to 1.8
- friend_accum: float32 [32768], P(('blk', 'grp')), may hold values from 10 to 200
- item_factors: float32 [4096, 128], P('blk'), may hold values from -1.8 to 1.8
- item_accum: float32 [4096], P('blk'), may hold values from 10 to 200
- rating_values: bfloat16 [2, 1024, 128, 128], P(None, ('blk', 'grp')), may hold values from -4 to 4
- rating_masks: int32 [2, 1024, 10, 128], P(None, ('blk', 'grp')), may hold values from 0 to 16383, as said below
- rating_rows: int32 [2, 1024], P(None, ('blk', 'grp')), may hold values from 0 to 7, as said below
- rating_cols: int32 [2, 1024], P(None, ('blk', 'grp')), may hold values from 0 to 3, as said below
- rating_counts: int32 [2, 32], P(None, ('blk', 'grp')), may hold values from 1 to 32, as said below
- trust_values: bfloat16 [1536, 128, 128], P(('blk', 'grp')), may hold values from 0 to 1
- trust_masks: int32 [1536, 10, 128], P(('blk', 'grp')), may hold values from 0 to 16383, as said below
- trust_rows: int32 [1536], P(('blk', 'grp')), may hold values from 0 to 7, as said below
- trust_cols: int32 [1536], P(('blk', 'grp')), may hold values from 0 to 7, as said below
- trust_counts: int32 [32], P(('blk', 'grp')), may hold values from 1 to 48, as said below
Outputs:
- user_out: float32 [32768, 128], P(('blk', 'grp'))
- user_acc_out: float32 [32768], P(('blk', 'grp'))
- friend_out: float32 [32768, 128], P(('blk', 'grp'))
- friend_acc_out: float32 [32768], P(('blk', 'grp'))
- item_out: float32 [4096, 128], P(('blk', 'grp'))
- item_acc_out: float32 [4096], P(('blk', 'grp'))
Inputs may be any that keep to these rules, and one draw needn't show every extreme that they name: `rating_rows`: in each stratum and group the listed (row, column) tile pairs of all slots are distinct. `rating_cols`: see rating_rows. `rating_counts`: slots at or past the count are ignored; in each stratum some group has all 32 slots live. `rating_masks`: bit i of word w at column c marks row 14 w + i of the tile; bits of rows at or past 128 are zero. `trust_rows`: in each group the listed (row, column) tile pairs of all slots are distinct. `trust_cols`: see trust_rows. `trust_counts`: slots at or past the count are ignored; some group has all 48 slots live. `trust_masks`: bit i of word w at column c marks row 14 w + i of the tile; bits of rows at or past 128 are zero.
All inputs are finite; a program needn't handle non-finite values.
Results may differ from a plain program's by a relative error of at most 0.005.
Values may be sent and summed in bfloat16 or wider, within the bound.
A program may use at most 64 MiB of HBM per device.

v0:
```python
import functools

import jax
import jax.numpy as jnp
from jax import lax
from jax.experimental import pallas as pl
from jax.experimental.pallas import tpu as pltpu
from jax.sharding import PartitionSpec as P

learn_rate = 0.3
shrinkage = 0.02
word_bits = 14
MESH = pl.DeviceIdType.MESH
f32, bf16 = jnp.float32, jnp.bfloat16


def slot_table(tile_rows, tile_cols, live_total, row_tiles, col_tiles):
    slots = jnp.arange(tile_rows.shape[0], dtype=jnp.int32)
    places = jnp.arange(row_tiles * col_tiles, dtype=jnp.int32)
    hit = (tile_rows * col_tiles + tile_cols)[None, :] == places[:, None]
    hit = hit & (slots < live_total)[None, :]
    return jnp.sum(jnp.where(hit, slots + 1, 0), axis=1, dtype=jnp.int32)


def spread(words, edge):
    sub = lax.broadcasted_iota(jnp.int32, (8, words.shape[1]), 0)
    pieces = []
    for first in range(0, edge, 8):
        low, high = first // word_bits, (first + 7) // word_bits
        piece = jnp.broadcast_to(words[low : low + 1], sub.shape)
        if high != low:
            after = jnp.broadcast_to(words[high : high + 1], sub.shape)
            piece = jnp.where(sub < high * word_bits - first, piece, after)
        pieces.append(piece)
    return jnp.concatenate(pieces, axis=0)


def as_columns(row, edge):
    return jnp.broadcast_to(row, (edge, edge)).T


def row_update(factor, accum, gradient):
    new_accum = accum + jnp.mean(gradient * gradient, axis=-1, keepdims=True)
    return factor - learn_rate * gradient * lax.rsqrt(new_accum), new_accum


def strata_kernel(
    blocks, groups,
    table, user_accum, friend_accum, item_accum,
    user_hbm, friend_hbm, item_hbm, rate_values, rate_masks, trust_values, trust_masks,
    user_out, user_acc_out, friend_out, friend_acc_out, item_out, item_acc_out,
    user, user_acc, user_low, user_t, friend, friend_low, far_low, item, item_low, item_next,
    values_0, values_1, values_2, masks_0, masks_1, masks_2, bits, residual,
    part, gathered, share_low, ship, shipped, far_part, friend_part,
    load_sem, far_send, far_recv, part_send, part_recv, low_send, low_recv,
    ship_send, ship_recv, back_send, back_recv,
):
    b, g = lax.axis_index("blk"), lax.axis_index("grp")
    after = lax.rem(b + 1, blocks)
    before = lax.rem(b + blocks - 1, blocks)
    partner = lax.rem(b + blocks // 2, blocks)
    edge = bits.shape[0]
    wide = 2 * edge
    user_rows, item_rows, friend_rows = user.shape[0], item.shape[0], friend.shape[0]
    user_tiles, item_tiles = user_rows // edge, item_rows // edge
    friend_tiles = friend_rows // edge

    barrier = pltpu.get_barrier_semaphore()
    for step in range(1, groups):
        pl.semaphore_signal(
            barrier, inc=1, device_id=(b, lax.rem(g + step, groups)), device_id_type=MESH
        )
    for other in range(groups):
        pl.semaphore_signal(barrier, inc=1, device_id=(before, other), device_id_type=MESH)
    pl.semaphore_signal(barrier, inc=1, device_id=(partner, g), device_id_type=MESH)

    pairs = [
        (friend_hbm, friend), (user_hbm, user), (item_hbm, item),
        (rate_masks.at[0], masks_0), (rate_values.at[0], values_0),
        (rate_masks.at[1], masks_1), (rate_values.at[1], values_1),
        (trust_masks, masks_2), (trust_values, values_2),
    ]
    loads = [
        pltpu.make_async_copy(src, dst, load_sem.at[n]) for n, (src, dst) in enumerate(pairs)
    ]
    for load in loads:
        load.start()

    place = lax.broadcasted_iota(jnp.int32, bits.shape, 0)
    bits[...] = jnp.left_shift(jnp.ones_like(place), lax.rem(place, word_bits))

    loads[0].wait()
    friend_low[...] = friend[...].astype(bf16)
    pl.semaphore_wait(barrier, 2 * groups)
    far_copy = pltpu.make_async_remote_copy(
        src_ref=friend_low, dst_ref=far_low, send_sem=far_send, recv_sem=far_recv,
        device_id=(partner, g), device_id_type=MESH,
    )
    far_copy.start()

    def keep_user(rows, state):
        low = state.astype(bf16)
        user_low[rows, :] = low
        user_t[:, rows] = state.T.astype(bf16)

    def tile_rows(tile):
        return pl.ds(pl.multiple_of(tile * edge, edge), edge)

    loads[1].wait()

    def first_user(tile, carry):
        rows = tile_rows(tile)
        keep_user(rows, user[rows, :])
        user_acc[rows, :] = as_columns(user_accum[pl.ds(tile, 1), :], edge)
        return carry

    lax.fori_loop(0, user_tiles, first_user, 0)
    loads[2].wait()
    item_low[...] = item[...].astype(bf16)

    def right_products(right_low, values, masks, base, col_tiles, chunk):
        columns = pl.ds(chunk * wide, wide)

        def block(pair, carry):
            rows = pl.ds(pl.multiple_of(pair * wide, wide), wide)
            predict = lax.dot_general(
                user_low[rows, :], right_low[columns, :], (((1,), (1,)), ((), ())),
                preferred_element_type=f32,
            )
            for i in range(2):
                for k in range(2):
                    found = table[base + (2 * pair + i) * col_tiles + 2 * chunk + k]
                    slot = jnp.maximum(found - 1, 0)
                    words = masks[slot] * jnp.minimum(found, 1)
                    seen = (spread(words, edge) & bits[...]) != 0
                    error = (
                        values[slot].astype(f32)
                        - predict[i * edge : (i + 1) * edge, k * edge : (k + 1) * edge]
                    )
                    residual[tile_rows(2 * pair + i), pl.ds(chunk * wide + k * edge, edge)] = (
                        jnp.where(seen, error, 0.0).astype(bf16)
                    )
            return carry

        lax.fori_loop(0, user_tiles // 2, block, 0)
        return jnp.dot(user_t[...], residual[:, columns], preferred_element_type=f32)

    def update_users(right_low, width, finish):
        def block(tile, carry):
            rows = tile_rows(tile)
            product = jnp.dot(
                residual[rows, pl.ds(0, width)], right_low[...], preferred_element_type=f32
            )
            state = user[rows, :]
            state, accum = row_update(state, user_acc[rows, :], shrinkage * state - product)
            finish(tile, rows, state, accum)
            return carry

        lax.fori_loop(0, user_tiles, block, 0)

    def part_copy(stratum, owner, source):
        return pltpu.make_async_remote_copy(
            src_ref=part.at[stratum, owner], dst_ref=gathered.at[stratum, source],
            send_sem=part_send.at[stratum, owner], recv_sem=part_recv.at[stratum, source],
            device_id=(b, owner), device_id_type=MESH,
        )

    def send_parts(stratum, right_low, values, masks, base):
        for chunk in range(item_tiles // 2):
            product = right_products(right_low, values, masks, base, item_tiles, chunk)
            for k in range(2):
                owner = 2 * chunk + k
                piece = product[:, k * edge : (k + 1) * edge].T.astype(bf16)
                part[stratum, owner] = piece

                @pl.when(owner != g)
                def _():
                    part_copy(stratum, owner, g).start()

                @pl.when(owner == g)
                def _():
                    gathered[stratum, g] = piece

    def part_total(stratum):
        for source in range(groups):
            @pl.when(source != g)
            def _():
                part_copy(stratum, source, source).wait_recv()

        total = gathered[stratum, 0].astype(f32)
        for source in range(1, groups):
            total = total + gathered[stratum, source].astype(f32)
        return total

    loads[3].wait()
    loads[4].wait()
    send_parts(0, item_low, values_0, masks_0, 0)

    def middle_user(tile, rows, state, accum):
        user[rows, :] = state
        user_acc[rows, :] = accum
        keep_user(rows, state)

    update_users(item_low, item_rows, middle_user)

    share = item[tile_rows(g), :]
    share, share_acc = row_update(
        share, as_columns(item_accum[pl.ds(g, 1), :], edge), shrinkage * share - part_total(0)
    )
    share_low[...] = share.astype(bf16)
    low_copies = [
        pltpu.make_async_remote_copy(
            src_ref=share_low, dst_ref=item_next.at[tile_rows(g), :],
            send_sem=low_send.at[other], recv_sem=low_recv.at[g],
            device_id=(after, other), device_id_type=MESH,
        )
        for other in range(groups)
    ]
    for copy in low_copies:
        copy.start()
    ship[pl.ds(0, edge), :] = share
    ship[pl.ds(edge, 8), :] = share_acc.T[0:8, :]
    ship_copy = pltpu.make_async_remote_copy(
        src_ref=ship, dst_ref=shipped, send_sem=ship_send, recv_sem=ship_recv,
        device_id=(after, g), device_id_type=MESH,
    )
    ship_copy.start()

    for n in range(5, 9):
        loads[n].wait()
    for source in range(groups):
        pltpu.make_async_remote_copy(
            src_ref=share_low, dst_ref=item_next.at[pl.ds(source * edge, edge), :],
            send_sem=low_send.at[source], recv_sem=low_recv.at[source],
            device_id=(after, source), device_id_type=MESH,
        ).wait_recv()
    send_parts(1, item_next, values_1, masks_1, user_tiles * item_tiles)
    update_users(item_next, item_rows, middle_user)

    far_copy.wait_recv()

    def back_copy(chunk):
        rows = pl.ds(chunk * wide, wide)
        return pltpu.make_async_remote_copy(
            src_ref=far_part.at[rows, :], dst_ref=friend_part.at[rows, :],
            send_sem=back_send.at[chunk], recv_sem=back_recv.at[chunk],
            device_id=(partner, g), device_id_type=MESH,
        )

    for chunk in range(friend_tiles // 2):
        product = right_products(
            far_low, values_2, masks_2, 2 * user_tiles * item_tiles, friend_tiles, chunk
        )
        far_part[pl.ds(chunk * wide, wide), :] = product.T.astype(bf16)
        back_copy(chunk).start()

    def last_user(tile, rows, state, accum):
        user_out[rows, :] = state
        user_acc_out[pl.ds(tile, 1), :] = accum.T[0:1, :]

    update_users(far_low, friend_rows, last_user)

    ship_copy.wait_recv()
    share = shipped[pl.ds(0, edge), :]
    share_acc = as_columns(shipped[pl.ds(edge, 1), :], edge)
    share, share_acc = row_update(share, share_acc, shrinkage * share - part_total(1))
    item_out[...] = share
    item_acc_out[...] = share_acc.T[0:1, :]

    for chunk in range(friend_tiles // 2):
        back_copy(chunk).wait_recv()
        for k in range(2):
            tile = 2 * chunk + k
            rows = pl.ds(tile * edge, edge)
            state = friend[rows, :]
            gradient = shrinkage * state - friend_part[rows, :].astype(f32)
            accum = as_columns(friend_accum[pl.ds(tile, 1), :], edge)
            state, accum = row_update(state, accum, gradient)
            friend_out[rows, :] = state
            friend_acc_out[pl.ds(tile, 1), :] = accum.T[0:1, :]

    far_copy.wait_send()
    for stratum in range(2):
        for owner in range(groups):
            @pl.when(owner != g)
            def _():
                part_copy(stratum, owner, g).wait_send()
    for copy in low_copies:
        copy.wait_send()
    ship_copy.wait_send()
    for chunk in range(friend_tiles // 2):
        back_copy(chunk).wait_send()


def local(
    user_factors, user_accum, friend_factors, friend_accum, item_factors, item_accum,
    rating_values, rating_masks, rating_rows, rating_cols, rating_counts,
    trust_values, trust_masks, trust_rows, trust_cols, trust_counts,
):
    blocks, groups = lax.axis_size("blk"), lax.axis_size("grp")
    edge, rank = rating_values.shape[-1], user_factors.shape[-1]
    users, items, friends = (
        user_factors.shape[0], item_factors.shape[0], friend_factors.shape[0]
    )
    user_tiles, item_tiles, friend_tiles = users // edge, items // edge, friends // edge
    assert edge == rank and items == groups * edge and blocks > 2
    assert user_tiles % 2 == 0 and item_tiles % 2 == 0 and friend_tiles % 2 == 0
    table = jnp.concatenate(
        [
            slot_table(
                rating_rows[s], rating_cols[s], rating_counts[s, 0], user_tiles, item_tiles
            )
            for s in range(2)
        ]
        + [slot_table(trust_rows, trust_cols, trust_counts[0], user_tiles, friend_tiles)]
    )
    vmem = pl.BlockSpec(memory_space=pltpu.VMEM)
    anywhere = pl.BlockSpec(memory_space=pl.ANY)
    dma = pltpu.SemaphoreType.DMA
    flops = 6 * rank * users * (2 * items + friends)
    user_out, user_acc, friend_out, friend_acc, item_out, item_acc = pl.pallas_call(
        functools.partial(strata_kernel, blocks, groups),
        out_shape=[
            jax.ShapeDtypeStruct((users, rank), f32),
            jax.ShapeDtypeStruct((user_tiles, edge), f32),
            jax.ShapeDtypeStruct((friends, rank), f32),
            jax.ShapeDtypeStruct((friend_tiles, edge), f32),
            jax.ShapeDtypeStruct((edge, rank), f32),
            jax.ShapeDtypeStruct((1, edge), f32),
        ],
        in_specs=[pl.BlockSpec(memory_space=pltpu.SMEM)] + [vmem] * 3 + [anywhere] * 7,
        out_specs=[vmem] * 6,
        scratch_shapes=[
            pltpu.VMEM((users, rank), f32),
            pltpu.VMEM((users, edge), f32),
            pltpu.VMEM((users, rank), bf16),
            pltpu.VMEM((rank, users), bf16),
            pltpu.VMEM((friends, rank), f32),
            pltpu.VMEM((friends, rank), bf16),
            pltpu.VMEM((friends, rank), bf16),
            pltpu.VMEM((items, rank), f32),
            pltpu.VMEM((items, rank), bf16),
            pltpu.VMEM((items, rank), bf16),
            pltpu.VMEM(rating_values.shape[1:], bf16),
            pltpu.VMEM(rating_values.shape[1:], bf16),
            pltpu.VMEM(trust_values.shape, bf16),
            pltpu.VMEM(rating_masks.shape[1:], jnp.int32),
            pltpu.VMEM(rating_masks.shape[1:], jnp.int32),
            pltpu.VMEM(trust_masks.shape, jnp.int32),
            pltpu.VMEM((edge, edge), jnp.int32),
            pltpu.VMEM((users, max(items, friends)), bf16),
            pltpu.VMEM((2, groups, edge, rank), bf16),
            pltpu.VMEM((2, groups, edge, rank), bf16),
            pltpu.VMEM((edge, rank), bf16),
            pltpu.VMEM((edge + 8, rank), f32),
            pltpu.VMEM((edge + 8, rank), f32),
            pltpu.VMEM((friends, rank), bf16),
            pltpu.VMEM((friends, rank), bf16),
            dma((9,)),
            dma, dma,
            dma((2, groups)), dma((2, groups)),
            dma((groups,)), dma((groups,)),
            dma, dma,
            dma((friend_tiles // 2,)), dma((friend_tiles // 2,)),
        ],
        compiler_params=pltpu.CompilerParams(
            collective_id=0, has_side_effects=True, vmem_limit_bytes=48 * 1024 * 1024
        ),
        cost_estimate=pl.CostEstimate(
            flops=flops, bytes_accessed=8 * 1024 * 1024, transcendentals=0
        ),
        name="strata",
    )(
        table,
        user_accum.reshape(user_tiles, edge),
        friend_accum.reshape(friend_tiles, edge),
        item_accum.reshape(item_tiles, edge),
        user_factors, friend_factors, item_factors,
        rating_values, rating_masks, trust_values, trust_masks,
    )
    return (
        user_out, user_acc.reshape(-1), friend_out, friend_acc.reshape(-1),
        item_out, item_acc.reshape(-1),
    )


def solution(mesh):
    split = P(("blk", "grp"))
    second = P(None, ("blk", "grp"))
    return jax.shard_map(
        local,
        mesh=mesh,
        in_specs=(
            split, split, split, split, P("blk"), P("blk"),
            second, second, second, second, second,
            split, split, split, split, split,
        ),
        out_specs=(split,) * 6,
        check_vma=False,
    )
```

profile of v0, /device:TPU:0, one launch (start us, length us, event | category | flops | bytes accessed | tf_op | source)
XLA Modules:
  0.0 51.6 jit_solution(14070965620647669416)
XLA Ops:
  1.3 0.8 %add_bitcast_fusion = (s32[32]{0:T(128)S(1)}, s32[32]{0:T(128)S(1)}) fusion(s32[2,32]{1,0:T(2,128)} %param.25, s32[2,32]{1,0:T(2,128)} %param.24), kind=kLoop, calls=%fused_computation.14 | loop fusion | flops 128 | bytes 768 | tf_op jit(solution)/shard_map/eq | solution.py:20
  2.1 1.3 %fusion.3 = (s32[1,1]{0,1:T(1,128)}, s32[1,1]{0,1:T(1,128)}) fusion(s32[2,1]{0,1:T(1,128)} %param.26), kind=kLoop, calls=%fused_computation.18 | loop fusion | bytes 16 | tf_op jit(solution)/shard_map/slice | solution.py:311
  3.4 1.3 %iota_compare_fusion.4 = (pred[32]{0:T(512)(128)(4,1)S(1)}, pred[32]{0:T(512)(128)(4,1)S(1)}) fusion(s32[]{:T(128)} %bitcast.3, s32[]{:T(128)} %bitcast.1), kind=kLoop, calls=%fused_computation.13 | loop fusion | flops 64 | bytes 72 | tf_op jit(solution)/shard_map/lt | solution.py:21
  4.7 0.1 select_reduce_fusion.2
  4.8 0.7 %iota_add_fusion = (s32[48]{0:T(128)S(1)}, s32[48]{0:T(128)S(1)}) fusion(s32[48]{0:T(128)} %param.30, s32[48]{0:T(128)} %param.29), kind=kLoop, calls=%fused_computation.10 | loop fusion | flops 144 | bytes 768 | tf_op jit(solution)/shard_map/add | solution.py:22
  5.5 0.1 select_reduce_fusion
  5.6 0.1 pad_add_fusion.table
  5.7 1.0 %copy.25.trust_masks = s32[48,10,128]{2,1,0:T(8,128)S(1)} copy(s32[48,10,128]{2,0,1:T(8,128)} %param.28) | data formatting | bytes 491520 | tf_op args[12]
  6.7 1.2 %copy.24.rate_masks = s32[2,32,10,128]{3,2,1,0:T(8,128)S(1)} copy(s32[2,32,10,128]{3,1,2,0:T(8,128)} %param.23) | data formatting | bytes 655360 | tf_op args[7]
  7.9 0.0 copy-start
  7.9 1.4 %copy-done = bf16[48,128,128]{2,1,0:T(8,128)(2,1)S(1)} copy-done((bf16[48,128,128]{2,1,0:T(8,128)(2,1)S(1)}, bf16[48,128,128]{2,1,0:T(8,128)(2,1)}, u32[]{:S(2)}) %copy-start) | copy-done | bytes 1572888
  9.3 0.0 copy-start.1
  9.3 1.0 %copy-done.1 = f32[1024,128]{1,0:T(8,128)S(1)} copy-done((f32[1024,128]{1,0:T(8,128)S(1)}, f32[1024,128]{1,0:T(8,128)}, u32[]{:S(2)}) %copy-start.1) | copy-done | bytes 524312
  10.3 0.0 copy-start.2
  10.3 1.0 %copy-done.2 = f32[1024,128]{1,0:T(8,128)S(1)} copy-done((f32[1024,128]{1,0:T(8,128)S(1)}, f32[1024,128]{1,0:T(8,128)}, u32[]{:S(2)}) %copy-start.2) | copy-done | bytes 524312
  11.4 0.0 copy-start.3
  11.4 0.9 %copy-done.3 = f32[512,128]{1,0:T(8,128)S(1)} copy-done((f32[512,128]{1,0:T(8,128)S(1)}, f32[512,128]{1,0:T(8,128)}, u32[]{:S(2)}) %copy-start.3) | copy-done | bytes 262168
  12.3 0.0 copy-start.4
  12.3 0.7 %copy-done.4 = f32[1024]{0:T(1024)S(1)} copy-done((f32[1024]{0:T(1024)S(1)}, f32[1024]{0:T(1024)}, u32[]{:S(2)}) %copy-start.4) | copy-done | bytes 4120
  13.0 0.0 copy-start.5
  13.0 0.7 %copy-done.5 = f32[1024]{0:T(1024)S(1)} copy-done((f32[1024]{0:T(1024)S(1)}, f32[1024]{0:T(1024)}, u32[]{:S(2)}) %copy-start.5) | copy-done | bytes 4120
  13.7 0.0 copy-start.6
  13.7 0.7 %copy-done.6 = f32[512]{0:T(512)S(1)} copy-done((f32[512]{0:T(512)S(1)}, f32[512]{0:T(512)}, u32[]{:S(2)}) %copy-start.6) | copy-done | bytes 2072
  14.4 33.2 %strata.1 = (f32[1024,128]{1,0:T(8,128)S(1)}, f32[8,128]{1,0:T(8,128)S(1)}, f32[1024,128]{1,0:T(8,128)S(1)}, f32[8,128]{1,0:T(8,128)S(1)}, f32[128,128]{1,0:T(8,128)S(1)}, /*index=5*/f32[1,128]{1,0:T(1,128)S(1)}) custom-call(s32[128]{0:T(128)S(1)} %pad_add_fusion.table, f32[8,128]{1,0:T(8,128)S(1)} %bitcast.16, f32[8,128]{1,0:T(8,128)S(1)} %bitcast.17, ...), custom_call_target="tpu_custom_call" | custom-call | flops 1610612736 | bytes 8388608 | tf_op jit(solution)/shard_map/strata/pallas_call | solution.py:321
  47.6 0.8 %copy.33 = f32[1024,128]{1,0:T(8,128)} copy(f32[1024,128]{1,0:T(8,128)S(1)} %get-tuple-element.34) | data formatting | bytes 1048576
  48.4 0.6 %copy.34 = f32[1024]{0:T(1024)} copy(f32[1024]{0:T(1024)S(1)} %bitcast.15) | data formatting | bytes 8192
  49.0 0.8 %copy.35 = f32[1024,128]{1,0:T(8,128)} copy(f32[1024,128]{1,0:T(8,128)S(1)} %get-tuple-element.36) | data formatting | bytes 1048576
  49.8 0.6 %copy.36 = f32[1024]{0:T(1024)} copy(f32[1024]{0:T(1024)S(1)} %bitcast.14) | data formatting | bytes 8192
  50.4 0.6 %copy.37 = f32[128,128]{1,0:T(8,128)} copy(f32[128,128]{1,0:T(8,128)S(1)} %get-tuple-element.38) | data formatting | bytes 131072
  51.1 0.5 copy.38
  (2 shorter events, 0.0 us)
Async XLA Ops:
  7.9 1.4 %copy-start = (bf16[48,128,128]{2,1,0:T(8,128)(2,1)S(1)}, bf16[48,128,128]{2,1,0:T(8,128)(2,1)}, u32[]{:S(2)}) copy-start(bf16[48,128,128]{2,1,0:T(8,128)(2,1)} %trust_values.1) | copy-start | bytes 4718596
  9.3 1.0 %copy-start.1 = (f32[1024,128]{1,0:T(8,128)S(1)}, f32[1024,128]{1,0:T(8,128)}, u32[]{:S(2)}) copy-start(f32[1024,128]{1,0:T(8,128)} %user_hbm.1) | copy-start | bytes 1572868
  10.3 1.0 %copy-start.2 = (f32[1024,128]{1,0:T(8,128)S(1)}, f32[1024,128]{1,0:T(8,128)}, u32[]{:S(2)}) copy-start(f32[1024,128]{1,0:T(8,128)} %friend_hbm.1) | copy-start | bytes 1572868
  11.4 0.9 %copy-start.3 = (f32[512,128]{1,0:T(8,128)S(1)}, f32[512,128]{1,0:T(8,128)}, u32[]{:S(2)}) copy-start(f32[512,128]{1,0:T(8,128)} %item_hbm.1) | copy-start | bytes 786436
  12.3 0.7 %copy-start.4 = (f32[1024]{0:T(1024)S(1)}, f32[1024]{0:T(1024)}, u32[]{:S(2)}) copy-start(f32[1024]{0:T(1024)} %param.17) | copy-start | bytes 12292
  13.0 0.7 %copy-start.5 = (f32[1024]{0:T(1024)S(1)}, f32[1024]{0:T(1024)}, u32[]{:S(2)}) copy-start(f32[1024]{0:T(1024)} %param.19) | copy-start | bytes 12292
  13.7 0.7 %copy-start.6 = (f32[512]{0:T(512)S(1)}, f32[512]{0:T(512)}, u32[]{:S(2)}) copy-start(f32[512]{0:T(512)} %param.21) | copy-start | bytes 6148
where the time goes:
time: 52.1 us; the launch traced here: 51.6 us
  Pallas kernels  33.2 us (64%)
  local copies, waits for them, and re-layouts  13.9 us (27%)
  other arithmetic  3.05 us (6%)
  between operations  1.33 us (3%)
    pallas_call x1, Pallas kernels, local(): pl.pallas_call(functools.partial(strata_kernel, blocks, groups), out_shap...  33.2 us
    unnamed x22, local copies, waits for them, and re-layouts  12.6 us
    slice x1, local copies, waits for them, and re-layouts, local(): rating_counts[s, 0]  1.31 us
    lt x2, other arithmetic, slot_table(): hit = hit & (slots < live_total)[None, :]  1.3 us

commit v1 on v0

--- a/solution.py
+++ b/solution.py
@@ -14,22 +14,35 @@
 f32, bf16 = jnp.float32, jnp.bfloat16
 
 
-def slot_table(tile_rows, tile_cols, live_total, row_tiles, col_tiles):
-    slots = jnp.arange(tile_rows.shape[0], dtype=jnp.int32)
-    places = jnp.arange(row_tiles * col_tiles, dtype=jnp.int32)
-    hit = (tile_rows * col_tiles + tile_cols)[None, :] == places[:, None]
-    hit = hit & (slots < live_total)[None, :]
-    return jnp.sum(jnp.where(hit, slots + 1, 0), axis=1, dtype=jnp.int32)
+def slot_table(seats, tables, edge):
+    seats[...] = jnp.full_like(seats[...], -2 * edge)
+    for n, (rows, cols, count, across, _) in enumerate(tables):
+        place = rows * across + cols
+        slot = lax.broadcasted_iota(jnp.int32, place.shape, 1)
+        seats[n : n + 1, 0 : place.shape[1]] = jnp.where(slot < count, place, -2 * edge)
+    lane = lax.broadcasted_iota(jnp.int32, (edge, edge), 1)
+    sub = lax.broadcasted_iota(jnp.int32, (edge, edge), 0)
+    line = jnp.zeros((1, edge), jnp.int32)
+    base = 0
+    for n, (rows, _, _, _, places) in enumerate(tables):
+        hit = as_columns(seats[n : n + 1, :], edge) == lane - base
+        found = jnp.sum(jnp.where(hit, sub + 1, 0), axis=0, keepdims=True)
+        entry = jnp.where(found > 0, found - 1, rows.shape[1])
+        inside = (lane[0:1] >= base) & (lane[0:1] < base + places)
+        line = jnp.where(inside, entry, line)
+        base += places
+    assert base <= edge
+    return line
 
 
 def spread(words, edge):
-    sub = lax.broadcasted_iota(jnp.int32, (8, words.shape[1]), 0)
+    sub = lax.broadcasted_iota(jnp.int32, (8, words.shape[2]), 0)
     pieces = []
     for first in range(0, edge, 8):
         low, high = first // word_bits, (first + 7) // word_bits
-        piece = jnp.broadcast_to(words[low : low + 1], sub.shape)
+        piece = jnp.broadcast_to(words[low], sub.shape)
         if high != low:
-            after = jnp.broadcast_to(words[high : high + 1], sub.shape)
+            after = jnp.broadcast_to(words[high], sub.shape)
             piece = jnp.where(sub < high * word_bits - first, piece, after)
         pieces.append(piece)
     return jnp.concatenate(pieces, axis=0)
@@ -46,13 +59,17 @@
 
 def strata_kernel(
     blocks, groups,
-    table, user_accum, friend_accum, item_accum,
-    user_hbm, friend_hbm, item_hbm, rate_values, rate_masks, trust_values, trust_masks,
+    user_hbm, friend_hbm, item_hbm, user_accum_hbm, friend_accum_hbm, item_accum_hbm,
+    rate_rows_hbm, rate_cols_hbm, rate_counts_hbm,
+    trust_rows_hbm, trust_cols_hbm, trust_counts_hbm,
+    rate_values, rate_masks, trust_values, trust_masks,
     user_out, user_acc_out, friend_out, friend_acc_out, item_out, item_acc_out,
     user, user_acc, user_low, user_t, friend, friend_low, far_low, item, item_low, item_next,
     values_0, values_1, values_2, masks_0, masks_1, masks_2, bits, residual,
-    part, gathered, share_low, ship, shipped, far_part, friend_part,
-    load_sem, far_send, far_recv, part_send, part_recv, low_send, low_recv,
+    user_accum, friend_accum, item_accum,
+    rate_rows, rate_cols, rate_counts, trust_rows, trust_cols, trust_counts,
+    seats, line, table, part_0, part_1, gathered_0, gathered_1, share_low, ship, shipped, far_part, friend_part,
+    load_sem, table_sem, far_send, far_recv, part_send, part_recv, low_send, low_recv,
     ship_send, ship_recv, back_send, back_recv,
 ):
     b, g = lax.axis_index("blk"), lax.axis_index("grp")
@@ -74,11 +91,22 @@
         pl.semaphore_signal(barrier, inc=1, device_id=(before, other), device_id_type=MESH)
     pl.semaphore_signal(barrier, inc=1, device_id=(partner, g), device_id_type=MESH)
 
+    part, gathered = (part_0, part_1), (gathered_0, gathered_1)
+    rate_slots, trust_slots = values_0.shape[0], values_2.shape[0]
     pairs = [
-        (friend_hbm, friend), (user_hbm, user), (item_hbm, item),
-        (rate_masks.at[0], masks_0), (rate_values.at[0], values_0),
-        (rate_masks.at[1], masks_1), (rate_values.at[1], values_1),
-        (trust_masks, masks_2), (trust_values, values_2),
+        (friend_hbm, friend),
+        (rate_rows_hbm, rate_rows), (rate_cols_hbm, rate_cols), (rate_counts_hbm, rate_counts),
+        (trust_rows_hbm, trust_rows), (trust_cols_hbm, trust_cols),
+        (trust_counts_hbm, trust_counts),
+        (user_accum_hbm, user_accum), (friend_accum_hbm, friend_accum),
+        (item_accum_hbm, item_accum),
+        (user_hbm, user), (item_hbm, item),
+        (rate_masks.at[0], masks_0.at[:, pl.ds(0, rate_slots), :]),
+        (rate_values.at[0], values_0),
+        (rate_masks.at[1], masks_1.at[:, pl.ds(0, rate_slots), :]),
+        (rate_values.at[1], values_1),
+        (trust_masks, masks_2.at[:, pl.ds(0, trust_slots), :]),
+        (trust_values, values_2),
     ]
     loads = [
         pltpu.make_async_copy(src, dst, load_sem.at[n]) for n, (src, dst) in enumerate(pairs)
@@ -88,6 +116,10 @@
 
     place = lax.broadcasted_iota(jnp.int32, bits.shape, 0)
     bits[...] = jnp.left_shift(jnp.ones_like(place), lax.rem(place, word_bits))
+
+    for masks in (masks_0, masks_1, masks_2):
+        spare = masks.shape[1] - 8
+        masks[:, pl.ds(spare, 8), :] = jnp.zeros((masks.shape[0], 8, edge), jnp.int32)
 
     loads[0].wait()
     friend_low[...] = friend[...].astype(bf16)
@@ -98,69 +130,73 @@
     )
     far_copy.start()
 
-    def keep_user(rows, state):
-        low = state.astype(bf16)
-        user_low[rows, :] = low
-        user_t[:, rows] = state.T.astype(bf16)
+    for n in range(1, 12):
+        loads[n].wait()
+    tables = [
+        (
+            rate_rows[s : s + 1, :], rate_cols[s : s + 1, :], rate_counts[:, s : s + 1],
+            item_tiles, user_tiles * item_tiles,
+        )
+        for s in range(2)
+    ]
+    tables.append(
+        (
+            trust_rows[...], trust_cols[...], trust_counts[...],
+            friend_tiles, user_tiles * friend_tiles,
+        )
+    )
+    line[...] = jnp.broadcast_to(slot_table(seats, tables, edge), line.shape)
+    table_copy = pltpu.make_async_copy(line, table, table_sem)
+    table_copy.start()
 
     def tile_rows(tile):
         return pl.ds(pl.multiple_of(tile * edge, edge), edge)
 
-    loads[1].wait()
-
-    def first_user(tile, carry):
-        rows = tile_rows(tile)
+    def keep_user(rows, state):
+        user_low[rows, :] = state.astype(bf16)
+        user_t[:, rows] = state.T.astype(bf16)
+
+    for tile in range(user_tiles):
+        rows = pl.ds(tile * edge, edge)
         keep_user(rows, user[rows, :])
         user_acc[rows, :] = as_columns(user_accum[pl.ds(tile, 1), :], edge)
-        return carry
-
-    lax.fori_loop(0, user_tiles, first_user, 0)
-    loads[2].wait()
     item_low[...] = item[...].astype(bf16)
+    table_copy.wait()
 
     def right_products(right_low, values, masks, base, col_tiles, chunk):
         columns = pl.ds(chunk * wide, wide)
 
-        def block(pair, carry):
-            rows = pl.ds(pl.multiple_of(pair * wide, wide), wide)
+        for pair in range(user_tiles // 2):
             predict = lax.dot_general(
-                user_low[rows, :], right_low[columns, :], (((1,), (1,)), ((), ())),
-                preferred_element_type=f32,
+                user_low[pl.ds(pair * wide, wide), :], right_low[columns, :],
+                (((1,), (1,)), ((), ())), preferred_element_type=f32,
             )
             for i in range(2):
                 for k in range(2):
-                    found = table[base + (2 * pair + i) * col_tiles + 2 * chunk + k]
-                    slot = jnp.maximum(found - 1, 0)
-                    words = masks[slot] * jnp.minimum(found, 1)
-                    seen = (spread(words, edge) & bits[...]) != 0
+                    slot = table[0, base + (2 * pair + i) * col_tiles + 2 * chunk + k]
+                    seen = (spread(masks[:, pl.ds(slot, 1), :], edge) & bits[...]) != 0
                     error = (
-                        values[slot].astype(f32)
+                        values[jnp.minimum(slot, values.shape[0] - 1)].astype(f32)
                         - predict[i * edge : (i + 1) * edge, k * edge : (k + 1) * edge]
                     )
-                    residual[tile_rows(2 * pair + i), pl.ds(chunk * wide + k * edge, edge)] = (
-                        jnp.where(seen, error, 0.0).astype(bf16)
-                    )
-            return carry
-
-        lax.fori_loop(0, user_tiles // 2, block, 0)
+                    residual[
+                        pl.ds((2 * pair + i) * edge, edge), pl.ds(chunk * wide + k * edge, edge)
+                    ] = jnp.where(seen, error, 0.0).astype(bf16)
         return jnp.dot(user_t[...], residual[:, columns], preferred_element_type=f32)
 
     def update_users(right_low, width, finish):
-        def block(tile, carry):
-            rows = tile_rows(tile)
+        for pair in range(user_tiles // 2):
+            rows = pl.ds(pair * wide, wide)
             product = jnp.dot(
                 residual[rows, pl.ds(0, width)], right_low[...], preferred_element_type=f32
             )
             state = user[rows, :]
             state, accum = row_update(state, user_acc[rows, :], shrinkage * state - product)
-            finish(tile, rows, state, accum)
-            return carry
-
-        lax.fori_loop(0, user_tiles, block, 0)
+            finish(pair, rows, state, accum)
 
     def part_copy(stratum, owner, source):
         return pltpu.make_async_remote_copy(
-            src_ref=part.at[stratum, owner], dst_ref=gathered.at[stratum, source],
+            src_ref=part[stratum].at[owner], dst_ref=gathered[stratum].at[source],
             send_sem=part_send.at[stratum, owner], recv_sem=part_recv.at[stratum, source],
             device_id=(b, owner), device_id_type=MESH,
         )
@@ -170,8 +206,8 @@
             product = right_products(right_low, values, masks, base, item_tiles, chunk)
             for k in range(2):
                 owner = 2 * chunk + k
-                piece = product[:, k * edge : (k + 1) * edge].T.astype(bf16)
-                part[stratum, owner] = piece
+                piece = product[:, k * edge : (k + 1) * edge].T.astype(part[stratum].dtype)
+                part[stratum][owner] = piece
 
                 @pl.when(owner != g)
                 def _():
@@ -179,7 +215,7 @@
 
                 @pl.when(owner == g)
                 def _():
-                    gathered[stratum, g] = piece
+                    gathered[stratum][g] = piece
 
     def part_total(stratum):
         for source in range(groups):
@@ -187,16 +223,16 @@
             def _():
                 part_copy(stratum, source, source).wait_recv()
 
-        total = gathered[stratum, 0].astype(f32)
+        total = gathered[stratum][0].astype(f32)
         for source in range(1, groups):
-            total = total + gathered[stratum, source].astype(f32)
+            total = total + gathered[stratum][source].astype(f32)
         return total
 
-    loads[3].wait()
-    loads[4].wait()
+    loads[12].wait()
+    loads[13].wait()
     send_parts(0, item_low, values_0, masks_0, 0)
 
-    def middle_user(tile, rows, state, accum):
+    def middle_user(pair, rows, state, accum):
         user[rows, :] = state
         user_acc[rows, :] = accum
         keep_user(rows, state)
@@ -226,7 +262,7 @@
     )
     ship_copy.start()
 
-    for n in range(5, 9):
+    for n in range(14, len(loads)):
         loads[n].wait()
     for source in range(groups):
         pltpu.make_async_remote_copy(
@@ -254,9 +290,10 @@
         far_part[pl.ds(chunk * wide, wide), :] = product.T.astype(bf16)
         back_copy(chunk).start()
 
-    def last_user(tile, rows, state, accum):
+    def last_user(pair, rows, state, accum):
         user_out[rows, :] = state
-        user_acc_out[pl.ds(tile, 1), :] = accum.T[0:1, :]
+        for k in range(2):
+            user_acc_out[pl.ds(2 * pair + k, 1), :] = accum[k * edge : (k + 1) * edge].T[0:1, :]
 
     update_users(far_low, friend_rows, last_user)
 
@@ -292,6 +329,17 @@
         back_copy(chunk).wait_send()
 
 
+def finish_kernel(*refs):
+    count = len(refs) // 2
+    copies = [
+        pltpu.make_async_copy(refs[n], refs[count + n], refs[-1].at[n]) for n in range(count)
+    ]
+    for copy in copies:
+        copy.start()
+    for copy in copies:
+        copy.wait()
+
+
 def local(
     user_factors, user_accum, friend_factors, friend_accum, item_factors, item_accum,
     rating_values, rating_masks, rating_rows, rating_cols, rating_counts,
@@ -305,30 +353,24 @@
     user_tiles, item_tiles, friend_tiles = users // edge, items // edge, friends // edge
     assert edge == rank and items == groups * edge and blocks > 2
     assert user_tiles % 2 == 0 and item_tiles % 2 == 0 and friend_tiles % 2 == 0
-    table = jnp.concatenate(
-        [
-            slot_table(
-                rating_rows[s], rating_cols[s], rating_counts[s, 0], user_tiles, item_tiles
-            )
-            for s in range(2)
-        ]
-        + [slot_table(trust_rows, trust_cols, trust_counts[0], user_tiles, friend_tiles)]
-    )
     vmem = pl.BlockSpec(memory_space=pltpu.VMEM)
-    anywhere = pl.BlockSpec(memory_space=pl.ANY)
+    hbm = pl.BlockSpec(memory_space=pltpu.HBM)
     dma = pltpu.SemaphoreType.DMA
     flops = 6 * rank * users * (2 * items + friends)
-    user_out, user_acc, friend_out, friend_acc, item_out, item_acc = pl.pallas_call(
+    shapes = [
+        jax.ShapeDtypeStruct((users, rank), f32),
+        jax.ShapeDtypeStruct((user_tiles, edge), f32),
+        jax.ShapeDtypeStruct((friends, rank), f32),
+        jax.ShapeDtypeStruct((friend_tiles, edge), f32),
+        jax.ShapeDtypeStruct((edge, rank), f32),
+        jax.ShapeDtypeStruct((1, edge), f32),
+    ]
+    rate_slots, mask_words = rating_masks.shape[1:3]
+    trust_slots = trust_masks.shape[0]
+    results = pl.pallas_call(
         functools.partial(strata_kernel, blocks, groups),
-        out_shape=[
-            jax.ShapeDtypeStruct((users, rank), f32),
-            jax.ShapeDtypeStruct((user_tiles, edge), f32),
-            jax.ShapeDtypeStruct((friends, rank), f32),
-            jax.ShapeDtypeStruct((friend_tiles, edge), f32),
-            jax.ShapeDtypeStruct((edge, rank), f32),
-            jax.ShapeDtypeStruct((1, edge), f32),
-        ],
-        in_specs=[pl.BlockSpec(memory_space=pltpu.SMEM)] + [vmem] * 3 + [anywhere] * 7,
+        out_shape=shapes,
+        in_specs=[hbm] * 16,
         out_specs=[vmem] * 6,
         scratch_shapes=[
             pltpu.VMEM((users, rank), f32),
@@ -344,19 +386,33 @@
             pltpu.VMEM(rating_values.shape[1:], bf16),
             pltpu.VMEM(rating_values.shape[1:], bf16),
             pltpu.VMEM(trust_values.shape, bf16),
-            pltpu.VMEM(rating_masks.shape[1:], jnp.int32),
-            pltpu.VMEM(rating_masks.shape[1:], jnp.int32),
-            pltpu.VMEM(trust_masks.shape, jnp.int32),
+            pltpu.VMEM((mask_words, rate_slots + 8, edge), jnp.int32),
+            pltpu.VMEM((mask_words, rate_slots + 8, edge), jnp.int32),
+            pltpu.VMEM((mask_words, trust_slots + 8, edge), jnp.int32),
             pltpu.VMEM((edge, edge), jnp.int32),
             pltpu.VMEM((users, max(items, friends)), bf16),
-            pltpu.VMEM((2, groups, edge, rank), bf16),
-            pltpu.VMEM((2, groups, edge, rank), bf16),
+            pltpu.VMEM((user_tiles, edge), f32),
+            pltpu.VMEM((friend_tiles, edge), f32),
+            pltpu.VMEM((item_tiles, edge), f32),
+            pltpu.VMEM((2, rate_slots), jnp.int32),
+            pltpu.VMEM((2, rate_slots), jnp.int32),
+            pltpu.VMEM((1, 2), jnp.int32),
+            pltpu.VMEM((1, trust_slots), jnp.int32),
+            pltpu.VMEM((1, trust_slots), jnp.int32),
+            pltpu.VMEM((1, 1), jnp.int32),
+            pltpu.VMEM((8, edge), jnp.int32),
+            pltpu.VMEM((8, edge), jnp.int32),
+            pltpu.SMEM((8, edge), jnp.int32),
+            pltpu.VMEM((groups, edge, rank), f32),
+            pltpu.VMEM((groups, edge, rank), bf16),
+            pltpu.VMEM((groups, edge, rank), f32),
+            pltpu.VMEM((groups, edge, rank), bf16),
             pltpu.VMEM((edge, rank), bf16),
             pltpu.VMEM((edge + 8, rank), f32),
             pltpu.VMEM((edge + 8, rank), f32),
             pltpu.VMEM((friends, rank), bf16),
             pltpu.VMEM((friends, rank), bf16),
-            dma((9,)),
+            dma((18,)), dma,
             dma, dma,
             dma((2, groups)), dma((2, groups)),
             dma((groups,)), dma((groups,)),
@@ -364,23 +420,33 @@
             dma((friend_tiles // 2,)), dma((friend_tiles // 2,)),
         ],
         compiler_params=pltpu.CompilerParams(
-            collective_id=0, has_side_effects=True, vmem_limit_bytes=48 * 1024 * 1024
+            collective_id=0, has_side_effects=True, vmem_limit_bytes=58 * 1024 * 1024
         ),
         cost_estimate=pl.CostEstimate(
             flops=flops, bytes_accessed=8 * 1024 * 1024, transcendentals=0
         ),
         name="strata",
     )(
-        table,
+        user_factors, friend_factors, item_factors,
         user_accum.reshape(user_tiles, edge),
         friend_accum.reshape(friend_tiles, edge),
         item_accum.reshape(item_tiles, edge),
-        user_factors, friend_factors, item_factors,
-        rating_values, rating_masks, trust_values, trust_masks,
-    )
-    return (
-        user_out, user_acc.reshape(-1), friend_out, friend_acc.reshape(-1),
-        item_out, item_acc.reshape(-1),
+        rating_rows, rating_cols, rating_counts.T,
+        trust_rows.reshape(1, -1), trust_cols.reshape(1, -1), trust_counts.reshape(1, 1),
+        rating_values, rating_masks.transpose(0, 2, 1, 3),
+        trust_values, trust_masks.transpose(1, 0, 2),
+    )
+    results = pl.pallas_call(
+        finish_kernel,
+        out_shape=shapes,
+        in_specs=[hbm] * len(shapes),
+        out_specs=[hbm] * len(shapes),
+        scratch_shapes=[dma((len(shapes),))],
+        compiler_params=pltpu.CompilerParams(vmem_limit_bytes=58 * 1024 * 1024),
+        name="finish",
+    )(*results)
+    return tuple(
+        result.reshape(-1) if n % 2 else result for n, result in enumerate(results)
     )
 
 

time: 52.1 us -> 68.9 us (1.32)
  Pallas kernels: 33.2 us -> 67.5 us
  local copies, waits for them, and re-layouts: 13.9 us -> 0 us
  other arithmetic: 3.05 us -> 0 us
    pallas_call x0 -> x1, Pallas kernels: none -> 35.2 us  [local(): pl.pallas_call(finish_kernel, out_shape=shapes, in_specs=[hbm] * len(shap...]
    unnamed x22 -> x0, local copies, waits for them, and re-layouts: 12.6 us -> none
    slice x1 -> x0, local copies, waits for them, and re-layouts: 1.31 us -> none  [local(): rating_counts[s, 0]]
    lt x2 -> x0, other arithmetic: 1.3 us -> none  [slot_table(): hit = hit & (slots < live_total)[None, :]]
    pallas_call x1, Pallas kernels: 33.2 us -> 32.3 us  [local(): pl.pallas_call(functools.partial(strata_kernel, blocks, groups), out_shap...]
    eq x1 -> x0, other arithmetic: 0.76 us -> none  [slot_table(): hit = (tile_rows * col_tiles + tile_cols)[None, :] == places[:, None]]
where the time goes in v1:
time: 68.9 us; the launch traced here: 68.8 us
  Pallas kernels  67.5 us (98%)
  between operations  1.29 us (2%)
    pallas_call x1, Pallas kernels, local(): pl.pallas_call(finish_kernel, out_shape=shapes, in_specs=[hbm] * len(shap...  35.2 us
    pallas_call x1, Pallas kernels, local(): pl.pallas_call(functools.partial(strata_kernel, blocks, groups), out_shap...  32.3 us

profile of v1, /device:TPU:0, one launch (start us, length us, event | category | flops | bytes accessed | tf_op | source)
XLA Modules:
  0.0 68.8 jit_solution(15745196647215950614)
XLA Ops:
  1.3 32.3 %strata.1 = (f32[1024,128]{1,0:T(8,128)}, f32[8,128]{1,0:T(8,128)}, f32[1024,128]{1,0:T(8,128)}, f32[8,128]{1,0:T(8,128)}, f32[128,128]{1,0:T(8,128)}, /*index=5*/f32[1,128]{1,0:T(1,128)}) custom-call(f32[1024,128]{1,0:T(8,128)} %user_hbm.1, f32[1024,128]{1,0:T(8,128)} %friend_hbm.1, f32[512,128]{1,0:T(8,128)} %item_hbm.1, f32[8,128]{1,0:T(8,128)} %bitcast.15, ...), custom_call_target="tpu_custom_call" | custom-call | flops 1610612736 | bytes 8388608 | tf_op jit(solution)/shard_map/strata/pallas_call | solution.py:370
  33.6 35.2 %finish.1 = (f32[1024,128]{1,0:T(8,128)}, f32[8,128]{1,0:T(8,128)}, f32[1024,128]{1,0:T(8,128)}, f32[8,128]{1,0:T(8,128)}, f32[128,128]{1,0:T(8,128)}, /*index=5*/f32[1,128]{1,0:T(1,128)}) custom-call(f32[1024,128]{1,0:T(8,128)} %get-tuple-element.18.refs_0_, f32[8,128]{1,0:T(8,128)} %get-tuple-element.19.refs_1_, f32[1024,128]{1,0:T(8,128)} %get-tuple-element.20.refs_2_, ...), custom_call_target="tpu_custom_call" | custom-call | tf_op jit(solution)/shard_map/finish/pallas_call | solution.py:439

commit v2 on v1

--- a/solution.py
+++ b/solution.py
@@ -65,7 +65,8 @@
     rate_values, rate_masks, trust_values, trust_masks,
     user_out, user_acc_out, friend_out, friend_acc_out, item_out, item_acc_out,
     user, user_acc, user_low, user_t, friend, friend_low, far_low, item, item_low, item_next,
-    values_0, values_1, values_2, masks_0, masks_1, masks_2, bits, residual,
+    values_0, values_1, values_2, masks_0, masks_1, masks_2, bits,
+    residual, residual_1, residual_2, observed_1, observed_2, friend_acc,
     user_accum, friend_accum, item_accum,
     rate_rows, rate_cols, rate_counts, trust_rows, trust_cols, trust_counts,
     seats, line, table, part_0, part_1, gathered_0, gathered_1, share_low, ship, shipped, far_part, friend_part,
@@ -78,9 +79,9 @@
     partner = lax.rem(b + blocks // 2, blocks)
     edge = bits.shape[0]
     wide = 2 * edge
-    user_rows, item_rows, friend_rows = user.shape[0], item.shape[0], friend.shape[0]
-    user_tiles, item_tiles = user_rows // edge, item_rows // edge
-    friend_tiles = friend_rows // edge
+    user_tiles, item_tiles, friend_tiles = (
+        rows.shape[0] // edge for rows in (user, item, friend)
+    )
 
     barrier = pltpu.get_barrier_semaphore()
     for step in range(1, groups):
@@ -94,7 +95,6 @@
     part, gathered = (part_0, part_1), (gathered_0, gathered_1)
     rate_slots, trust_slots = values_0.shape[0], values_2.shape[0]
     pairs = [
-        (friend_hbm, friend),
         (rate_rows_hbm, rate_rows), (rate_cols_hbm, rate_cols), (rate_counts_hbm, rate_counts),
         (trust_rows_hbm, trust_rows), (trust_cols_hbm, trust_cols),
         (trust_counts_hbm, trust_counts),
@@ -103,6 +103,7 @@
         (user_hbm, user), (item_hbm, item),
         (rate_masks.at[0], masks_0.at[:, pl.ds(0, rate_slots), :]),
         (rate_values.at[0], values_0),
+        (friend_hbm, friend),
         (rate_masks.at[1], masks_1.at[:, pl.ds(0, rate_slots), :]),
         (rate_values.at[1], values_1),
         (trust_masks, masks_2.at[:, pl.ds(0, trust_slots), :]),
@@ -121,16 +122,12 @@
         spare = masks.shape[1] - 8
         masks[:, pl.ds(spare, 8), :] = jnp.zeros((masks.shape[0], 8, edge), jnp.int32)
 
-    loads[0].wait()
-    friend_low[...] = friend[...].astype(bf16)
-    pl.semaphore_wait(barrier, 2 * groups)
     far_copy = pltpu.make_async_remote_copy(
         src_ref=friend_low, dst_ref=far_low, send_sem=far_send, recv_sem=far_recv,
         device_id=(partner, g), device_id_type=MESH,
     )
-    far_copy.start()
-
-    for n in range(1, 12):
+
+    for n in range(11):
         loads[n].wait()
     tables = [
         (
@@ -163,32 +160,59 @@
     item_low[...] = item[...].astype(bf16)
     table_copy.wait()
 
-    def right_products(right_low, values, masks, base, col_tiles, chunk):
-        columns = pl.ds(chunk * wide, wide)
-
+    def tile_operands(values, masks, index):
+        slot = table[0, index]
+        seen = (spread(masks[:, pl.ds(slot, 1), :], edge) & bits[...]) != 0
+        return seen, values[jnp.minimum(slot, values.shape[0] - 1)]
+
+    def prepare(held, observed, values, masks, base, col_tiles):
+        for r in range(user_tiles):
+            for c in range(col_tiles):
+                seen, value = tile_operands(values, masks, base + r * col_tiles + c)
+                at = pl.ds(r * edge, edge), pl.ds(c * edge, edge)
+                held[at] = jnp.where(seen, value.astype(f32), 0.0).astype(bf16)
+                observed[at] = jnp.where(seen, 1.0, 0.0).astype(bf16)
+
+    def predicted(right_low, pair, columns):
+        return lax.dot_general(
+            user_low[pl.ds(pair * wide, wide), :], right_low[columns, :],
+            (((1,), (1,)), ((), ())), preferred_element_type=f32,
+        )
+
+    def direct_residual(right_low, values, masks, base, col_tiles, chunk):
         for pair in range(user_tiles // 2):
-            predict = lax.dot_general(
-                user_low[pl.ds(pair * wide, wide), :], right_low[columns, :],
-                (((1,), (1,)), ((), ())), preferred_element_type=f32,
-            )
+            predict = predicted(right_low, pair, pl.ds(chunk * wide, wide))
             for i in range(2):
                 for k in range(2):
-                    slot = table[0, base + (2 * pair + i) * col_tiles + 2 * chunk + k]
-                    seen = (spread(masks[:, pl.ds(slot, 1), :], edge) & bits[...]) != 0
-                    error = (
-                        values[jnp.minimum(slot, values.shape[0] - 1)].astype(f32)
-                        - predict[i * edge : (i + 1) * edge, k * edge : (k + 1) * edge]
+                    seen, value = tile_operands(
+                        values, masks, base + (2 * pair + i) * col_tiles + 2 * chunk + k
+                    )
+                    error = value.astype(f32) - (
+                        predict[i * edge : (i + 1) * edge, k * edge : (k + 1) * edge]
                     )
                     residual[
                         pl.ds((2 * pair + i) * edge, edge), pl.ds(chunk * wide + k * edge, edge)
                     ] = jnp.where(seen, error, 0.0).astype(bf16)
-        return jnp.dot(user_t[...], residual[:, columns], preferred_element_type=f32)
-
-    def update_users(right_low, width, finish):
+
+    def prepared_residual(right_low, observed, held, chunk):
+        columns = pl.ds(chunk * wide, wide)
+        for pair in range(user_tiles // 2):
+            rows = pl.ds(pair * wide, wide)
+            predict = predicted(right_low, pair, columns)
+            held[rows, columns] = (
+                held[rows, columns].astype(f32) - observed[rows, columns].astype(f32) * predict
+            ).astype(bf16)
+
+    def right_products(held, chunk):
+        return jnp.dot(
+            user_t[...], held[:, pl.ds(chunk * wide, wide)], preferred_element_type=f32
+        )
+
+    def update_users(right_low, held, finish):
         for pair in range(user_tiles // 2):
             rows = pl.ds(pair * wide, wide)
             product = jnp.dot(
-                residual[rows, pl.ds(0, width)], right_low[...], preferred_element_type=f32
+                held[rows, :], right_low[...], preferred_element_type=f32
             )
             state = user[rows, :]
             state, accum = row_update(state, user_acc[rows, :], shrinkage * state - product)
@@ -201,21 +225,20 @@
             device_id=(b, owner), device_id_type=MESH,
         )
 
-    def send_parts(stratum, right_low, values, masks, base):
-        for chunk in range(item_tiles // 2):
-            product = right_products(right_low, values, masks, base, item_tiles, chunk)
-            for k in range(2):
-                owner = 2 * chunk + k
-                piece = product[:, k * edge : (k + 1) * edge].T.astype(part[stratum].dtype)
-                part[stratum][owner] = piece
-
-                @pl.when(owner != g)
-                def _():
-                    part_copy(stratum, owner, g).start()
-
-                @pl.when(owner == g)
-                def _():
-                    gathered[stratum][g] = piece
+    def send_parts(stratum, held, chunk):
+        product = right_products(held, chunk)
+        for k in range(2):
+            owner = 2 * chunk + k
+            piece = product[:, k * edge : (k + 1) * edge].T.astype(part[stratum].dtype)
+            part[stratum][owner] = piece
+
+            @pl.when(owner != g)
+            def _():
+                part_copy(stratum, owner, g).start()
+
+            @pl.when(owner == g)
+            def _():
+                gathered[stratum][g] = piece
 
     def part_total(stratum):
         for source in range(groups):
@@ -228,16 +251,27 @@
             total = total + gathered[stratum][source].astype(f32)
         return total
 
+    loads[11].wait()
     loads[12].wait()
+    for chunk in range(item_tiles // 2):
+        direct_residual(item_low, values_0, masks_0, 0, item_tiles, chunk)
+        if chunk == 0:
+            pl.semaphore_wait(barrier, 2 * groups)
+        send_parts(0, residual, chunk)
+
     loads[13].wait()
-    send_parts(0, item_low, values_0, masks_0, 0)
+    friend_low[...] = friend[...].astype(bf16)
+    far_copy.start()
 
     def middle_user(pair, rows, state, accum):
         user[rows, :] = state
         user_acc[rows, :] = accum
         keep_user(rows, state)
 
-    update_users(item_low, item_rows, middle_user)
+    update_users(item_low, residual, middle_user)
+    loads[14].wait()
+    loads[15].wait()
+    prepare(residual_1, observed_1, values_1, masks_1, user_tiles * item_tiles, item_tiles)
 
     share = item[tile_rows(g), :]
     share, share_acc = row_update(
@@ -262,16 +296,25 @@
     )
     ship_copy.start()
 
-    for n in range(14, len(loads)):
-        loads[n].wait()
+    loads[16].wait()
+    loads[17].wait()
+    prepare(
+        residual_2, observed_2, values_2, masks_2, 2 * user_tiles * item_tiles, friend_tiles
+    )
+    for tile in range(friend_tiles):
+        friend_acc[pl.ds(tile * edge, edge), :] = as_columns(
+            friend_accum[pl.ds(tile, 1), :], edge
+        )
     for source in range(groups):
         pltpu.make_async_remote_copy(
             src_ref=share_low, dst_ref=item_next.at[pl.ds(source * edge, edge), :],
             send_sem=low_send.at[source], recv_sem=low_recv.at[source],
             device_id=(after, source), device_id_type=MESH,
         ).wait_recv()
-    send_parts(1, item_next, values_1, masks_1, user_tiles * item_tiles)
-    update_users(item_next, item_rows, middle_user)
+    for chunk in range(item_tiles // 2):
+        prepared_residual(item_next, observed_1, residual_1, chunk)
+        send_parts(1, residual_1, chunk)
+    update_users(item_next, residual_1, middle_user)
 
     far_copy.wait_recv()
 
@@ -284,9 +327,8 @@
         )
 
     for chunk in range(friend_tiles // 2):
-        product = right_products(
-            far_low, values_2, masks_2, 2 * user_tiles * item_tiles, friend_tiles, chunk
-        )
+        prepared_residual(far_low, observed_2, residual_2, chunk)
+        product = right_products(residual_2, chunk)
         far_part[pl.ds(chunk * wide, wide), :] = product.T.astype(bf16)
         back_copy(chunk).start()
 
@@ -295,7 +337,7 @@
         for k in range(2):
             user_acc_out[pl.ds(2 * pair + k, 1), :] = accum[k * edge : (k + 1) * edge].T[0:1, :]
 
-    update_users(far_low, friend_rows, last_user)
+    update_users(far_low, residual_2, last_user)
 
     ship_copy.wait_recv()
     share = shipped[pl.ds(0, edge), :]
@@ -311,8 +353,7 @@
             rows = pl.ds(tile * edge, edge)
             state = friend[rows, :]
             gradient = shrinkage * state - friend_part[rows, :].astype(f32)
-            accum = as_columns(friend_accum[pl.ds(tile, 1), :], edge)
-            state, accum = row_update(state, accum, gradient)
+            state, accum = row_update(state, friend_acc[rows, :], gradient)
             friend_out[rows, :] = state
             friend_acc_out[pl.ds(tile, 1), :] = accum.T[0:1, :]
 
@@ -329,14 +370,20 @@
         back_copy(chunk).wait_send()
 
 
-def finish_kernel(*refs):
-    count = len(refs) // 2
-    copies = [
-        pltpu.make_async_copy(refs[n], refs[count + n], refs[-1].at[n]) for n in range(count)
-    ]
-    for copy in copies:
+def finish_kernel(count, *refs):
+    sources, targets, held = refs[:count], refs[count : 2 * count], refs[2 * count : -2]
+    fills = [
+        pltpu.make_async_copy(sources[n], held[n], refs[-2].at[n]) for n in range(count)
+    ]
+    drains = [
+        pltpu.make_async_copy(held[n], targets[n], refs[-1].at[n]) for n in range(count)
+    ]
+    for copy in fills:
         copy.start()
-    for copy in copies:
+    for fill, drain in zip(fills, drains):
+        fill.wait()
+        drain.start()
+    for copy in drains:
         copy.wait()
 
 
@@ -390,7 +437,12 @@
             pltpu.VMEM((mask_words, rate_slots + 8, edge), jnp.int32),
             pltpu.VMEM((mask_words, trust_slots + 8, edge), jnp.int32),
             pltpu.VMEM((edge, edge), jnp.int32),
-            pltpu.VMEM((users, max(items, friends)), bf16),
+            pltpu.VMEM((users, items), bf16),
+            pltpu.VMEM((users, items), bf16),
+            pltpu.VMEM((users, friends), bf16),
+            pltpu.VMEM((users, items), bf16),
+            pltpu.VMEM((users, friends), bf16),
+            pltpu.VMEM((friends, edge), f32),
             pltpu.VMEM((user_tiles, edge), f32),
             pltpu.VMEM((friend_tiles, edge), f32),
             pltpu.VMEM((item_tiles, edge), f32),
@@ -437,11 +489,12 @@
         trust_values, trust_masks.transpose(1, 0, 2),
     )
     results = pl.pallas_call(
-        finish_kernel,
+        functools.partial(finish_kernel, len(shapes)),
         out_shape=shapes,
         in_specs=[hbm] * len(shapes),
         out_specs=[hbm] * len(shapes),
-        scratch_shapes=[dma((len(shapes),))],
+        scratch_shapes=[pltpu.VMEM(shape.shape, shape.dtype) for shape in shapes]
+        + [dma((len(shapes),)), dma((len(shapes),))],
         compiler_params=pltpu.CompilerParams(vmem_limit_bytes=58 * 1024 * 1024),
         name="finish",
     )(*results)

time: 68.9 us -> 34.5 us (0.50)
  Pallas kernels: 67.5 us -> 33 us
    pallas_call x1, Pallas kernels: 35.2 us -> 2.13 us  [local(): pl.pallas_call(functools.partial(finish_kernel, len(shapes)), out_shape=s...]
    pallas_call x1, Pallas kernels: 32.3 us -> 30.9 us  [local(): pl.pallas_call(functools.partial(strata_kernel, blocks, groups), out_shap...]
where the time goes in v2:
time: 34.5 us; the launch traced here: 34.3 us
  Pallas kernels  33 us (96%)
  between operations  1.29 us (4%)
    pallas_call x1, Pallas kernels, local(): pl.pallas_call(functools.partial(strata_kernel, blocks, groups), out_shap...  30.9 us
    pallas_call x1, Pallas kernels, local(): pl.pallas_call(functools.partial(finish_kernel, len(shapes)), out_shape=s...  2.13 us

profile of v2, /device:TPU:0, one launch (start us, length us, event | category | flops | bytes accessed | tf_op | source)
XLA Modules:
  0.0 34.3 jit_solution(12677134373982935940)
XLA Ops:
  1.3 30.9 %strata.1 = (f32[1024,128]{1,0:T(8,128)}, f32[8,128]{1,0:T(8,128)}, f32[1024,128]{1,0:T(8,128)}, f32[8,128]{1,0:T(8,128)}, f32[128,128]{1,0:T(8,128)}, /*index=5*/f32[1,128]{1,0:T(1,128)}) custom-call(f32[1024,128]{1,0:T(8,128)} %user_hbm.1, f32[1024,128]{1,0:T(8,128)} %friend_hbm.1, f32[512,128]{1,0:T(8,128)} %item_hbm.1, f32[8,128]{1,0:T(8,128)} %bitcast.15, ...), custom_call_target="tpu_custom_call" | custom-call | flops 1610612736 | bytes 8388608 | tf_op jit(solution)/shard_map/strata/pallas_call | solution.py:417
  32.2 2.1 %finish.1 = (f32[1024,128]{1,0:T(8,128)}, f32[8,128]{1,0:T(8,128)}, f32[1024,128]{1,0:T(8,128)}, f32[8,128]{1,0:T(8,128)}, f32[128,128]{1,0:T(8,128)}, /*index=5*/f32[1,128]{1,0:T(1,128)}) custom-call(f32[1024,128]{1,0:T(8,128)} %get-tuple-element.18.refs_0_, f32[8,128]{1,0:T(8,128)} %get-tuple-element.19.refs_1_, f32[1024,128]{1,0:T(8,128)} %get-tuple-element.20.refs_2_, ...), custom_call_target="tpu_custom_call" | custom-call | tf_op jit(solution)/shard_map/finish/pallas_call | solution.py:491

commit v3 on v2

--- a/solution.py
+++ b/solution.py
@@ -64,13 +64,14 @@
     trust_rows_hbm, trust_cols_hbm, trust_counts_hbm,
     rate_values, rate_masks, trust_values, trust_masks,
     user_out, user_acc_out, friend_out, friend_acc_out, item_out, item_acc_out,
-    user, user_acc, user_low, user_t, friend, friend_low, far_low, item, item_low, item_next,
+    user, user_acc, user_low, user_t, user_t_last, friend, friend_low, far_low, item, item_low, item_next,
     values_0, values_1, values_2, masks_0, masks_1, masks_2, bits,
     residual, residual_1, residual_2, observed_1, observed_2, friend_acc,
     user_accum, friend_accum, item_accum,
     rate_rows, rate_cols, rate_counts, trust_rows, trust_cols, trust_counts,
-    seats, line, table, part_0, part_1, gathered_0, gathered_1, share_low, ship, shipped, far_part, friend_part,
-    load_sem, table_sem, far_send, far_recv, part_send, part_recv, low_send, low_recv,
+    seats, line, table, part_0, part_1, gathered_0, gathered_1, share_end, share_acc_end,
+    share_low, ship, shipped, far_part, friend_part,
+    load_sem, store_sem, table_sem, far_send, far_recv, part_send, part_recv, low_send, low_recv,
     ship_send, ship_recv, back_send, back_recv,
 ):
     b, g = lax.axis_index("blk"), lax.axis_index("grp")
@@ -112,7 +113,7 @@
     loads = [
         pltpu.make_async_copy(src, dst, load_sem.at[n]) for n, (src, dst) in enumerate(pairs)
     ]
-    for load in loads:
+    for load in loads[:13]:
         load.start()
 
     place = lax.broadcasted_iota(jnp.int32, bits.shape, 0)
@@ -149,13 +150,13 @@
     def tile_rows(tile):
         return pl.ds(pl.multiple_of(tile * edge, edge), edge)
 
-    def keep_user(rows, state):
+    def keep_user(target_t, rows, state):
         user_low[rows, :] = state.astype(bf16)
-        user_t[:, rows] = state.T.astype(bf16)
+        target_t[:, rows] = state.T.astype(bf16)
 
     for tile in range(user_tiles):
         rows = pl.ds(tile * edge, edge)
-        keep_user(rows, user[rows, :])
+        keep_user(user_t, rows, user[rows, :])
         user_acc[rows, :] = as_columns(user_accum[pl.ds(tile, 1), :], edge)
     item_low[...] = item[...].astype(bf16)
     table_copy.wait()
@@ -164,6 +165,9 @@
         slot = table[0, index]
         seen = (spread(masks[:, pl.ds(slot, 1), :], edge) & bits[...]) != 0
         return seen, values[jnp.minimum(slot, values.shape[0] - 1)]
+
+    def wide_columns(chunk):
+        return pl.ds(pl.multiple_of(chunk * wide, wide), wide)
 
     def prepare(held, observed, values, masks, base, col_tiles):
         for r in range(user_tiles):
@@ -181,7 +185,7 @@
 
     def direct_residual(right_low, values, masks, base, col_tiles, chunk):
         for pair in range(user_tiles // 2):
-            predict = predicted(right_low, pair, pl.ds(chunk * wide, wide))
+            predict = predicted(right_low, pair, wide_columns(chunk))
             for i in range(2):
                 for k in range(2):
                     seen, value = tile_operands(
@@ -191,11 +195,12 @@
                         predict[i * edge : (i + 1) * edge, k * edge : (k + 1) * edge]
                     )
                     residual[
-                        pl.ds((2 * pair + i) * edge, edge), pl.ds(chunk * wide + k * edge, edge)
+                        pl.ds((2 * pair + i) * edge, edge),
+                        pl.ds(pl.multiple_of(chunk * wide + k * edge, edge), edge),
                     ] = jnp.where(seen, error, 0.0).astype(bf16)
 
     def prepared_residual(right_low, observed, held, chunk):
-        columns = pl.ds(chunk * wide, wide)
+        columns = wide_columns(chunk)
         for pair in range(user_tiles // 2):
             rows = pl.ds(pair * wide, wide)
             predict = predicted(right_low, pair, columns)
@@ -203,9 +208,9 @@
                 held[rows, columns].astype(f32) - observed[rows, columns].astype(f32) * predict
             ).astype(bf16)
 
-    def right_products(held, chunk):
+    def right_products(left_t, held, chunk):
         return jnp.dot(
-            user_t[...], held[:, pl.ds(chunk * wide, wide)], preferred_element_type=f32
+            left_t[...], held[:, wide_columns(chunk)], preferred_element_type=f32
         )
 
     def update_users(right_low, held, finish):
@@ -225,8 +230,8 @@
             device_id=(b, owner), device_id_type=MESH,
         )
 
-    def send_parts(stratum, held, chunk):
-        product = right_products(held, chunk)
+    def send_parts(stratum, left_t, held, chunk):
+        product = right_products(left_t, held, chunk)
         for k in range(2):
             owner = 2 * chunk + k
             piece = product[:, k * edge : (k + 1) * edge].T.astype(part[stratum].dtype)
@@ -253,22 +258,30 @@
 
     loads[11].wait()
     loads[12].wait()
-    for chunk in range(item_tiles // 2):
+    for load in loads[13:]:
+        load.start()
+    chunks = item_tiles // 2
+    near = lax.div(g, 2)
+    for step in range(chunks):
+        chunk = lax.rem(near + 1 + step, chunks)
         direct_residual(item_low, values_0, masks_0, 0, item_tiles, chunk)
-        if chunk == 0:
+        if step == 0:
             pl.semaphore_wait(barrier, 2 * groups)
-        send_parts(0, residual, chunk)
+        send_parts(0, user_t, residual, chunk)
 
     loads[13].wait()
     friend_low[...] = friend[...].astype(bf16)
     far_copy.start()
 
-    def middle_user(pair, rows, state, accum):
-        user[rows, :] = state
-        user_acc[rows, :] = accum
-        keep_user(rows, state)
-
-    update_users(item_low, residual, middle_user)
+    def middle_user(target_t):
+        def finish(pair, rows, state, accum):
+            user[rows, :] = state
+            user_acc[rows, :] = accum
+            keep_user(target_t, rows, state)
+
+        return finish
+
+    update_users(item_low, residual, middle_user(user_t))
     loads[14].wait()
     loads[15].wait()
     prepare(residual_1, observed_1, values_1, masks_1, user_tiles * item_tiles, item_tiles)
@@ -281,10 +294,10 @@
     low_copies = [
         pltpu.make_async_remote_copy(
             src_ref=share_low, dst_ref=item_next.at[tile_rows(g), :],
-            send_sem=low_send.at[other], recv_sem=low_recv.at[g],
-            device_id=(after, other), device_id_type=MESH,
-        )
-        for other in range(groups)
+            send_sem=low_send.at[step], recv_sem=low_recv.at[g],
+            device_id=(after, lax.rem(g + groups // 2 + step, groups)), device_id_type=MESH,
+        )
+        for step in range(groups)
     ]
     for copy in low_copies:
         copy.start()
@@ -305,16 +318,17 @@
         friend_acc[pl.ds(tile * edge, edge), :] = as_columns(
             friend_accum[pl.ds(tile, 1), :], edge
         )
-    for source in range(groups):
-        pltpu.make_async_remote_copy(
-            src_ref=share_low, dst_ref=item_next.at[pl.ds(source * edge, edge), :],
-            send_sem=low_send.at[source], recv_sem=low_recv.at[source],
-            device_id=(after, source), device_id_type=MESH,
-        ).wait_recv()
-    for chunk in range(item_tiles // 2):
+    for step in range(chunks):
+        chunk = lax.rem(near + step, chunks)
+        for k in range(2):
+            source = 2 * chunk + k
+            pltpu.make_async_remote_copy(
+                src_ref=share_low, dst_ref=item_next.at[tile_rows(source), :],
+                send_sem=low_send.at[source], recv_sem=low_recv.at[source],
+                device_id=(after, source), device_id_type=MESH,
+            ).wait_recv()
         prepared_residual(item_next, observed_1, residual_1, chunk)
-        send_parts(1, residual_1, chunk)
-    update_users(item_next, residual_1, middle_user)
+    update_users(item_next, residual_1, middle_user(user_t_last))
 
     far_copy.wait_recv()
 
@@ -328,23 +342,35 @@
 
     for chunk in range(friend_tiles // 2):
         prepared_residual(far_low, observed_2, residual_2, chunk)
-        product = right_products(residual_2, chunk)
+        product = right_products(user_t_last, residual_2, chunk)
         far_part[pl.ds(chunk * wide, wide), :] = product.T.astype(bf16)
         back_copy(chunk).start()
+        if chunk < chunks:
+            send_parts(1, user_t, residual_1, chunk)
 
     def last_user(pair, rows, state, accum):
-        user_out[rows, :] = state
+        user[rows, :] = state
         for k in range(2):
-            user_acc_out[pl.ds(2 * pair + k, 1), :] = accum[k * edge : (k + 1) * edge].T[0:1, :]
+            user_accum[pl.ds(2 * pair + k, 1), :] = accum[k * edge : (k + 1) * edge].T[0:1, :]
 
     update_users(far_low, residual_2, last_user)
+    stores = [
+        pltpu.make_async_copy(user, user_out, store_sem.at[0]),
+        pltpu.make_async_copy(user_accum, user_acc_out, store_sem.at[1]),
+    ]
+    for store in stores:
+        store.start()
 
     ship_copy.wait_recv()
     share = shipped[pl.ds(0, edge), :]
     share_acc = as_columns(shipped[pl.ds(edge, 1), :], edge)
     share, share_acc = row_update(share, share_acc, shrinkage * share - part_total(1))
-    item_out[...] = share
-    item_acc_out[...] = share_acc.T[0:1, :]
+    share_end[...] = share
+    share_acc_end[...] = share_acc.T[0:1, :]
+    ends = [(share_end, item_out), (share_acc_end, item_acc_out)]
+    for src, dst in ends:
+        stores.append(pltpu.make_async_copy(src, dst, store_sem.at[len(stores)]))
+        stores[-1].start()
 
     for chunk in range(friend_tiles // 2):
         back_copy(chunk).wait_recv()
@@ -354,9 +380,22 @@
             state = friend[rows, :]
             gradient = shrinkage * state - friend_part[rows, :].astype(f32)
             state, accum = row_update(state, friend_acc[rows, :], gradient)
-            friend_out[rows, :] = state
-            friend_acc_out[pl.ds(tile, 1), :] = accum.T[0:1, :]
-
+            friend[rows, :] = state
+            friend_accum[pl.ds(tile, 1), :] = accum.T[0:1, :]
+        rows = pl.ds(chunk * wide, wide)
+        stores.append(
+            pltpu.make_async_copy(
+                friend.at[rows, :], friend_out.at[rows, :], store_sem.at[len(stores)]
+            )
+        )
+        stores[-1].start()
+    stores.append(
+        pltpu.make_async_copy(friend_accum, friend_acc_out, store_sem.at[len(stores)])
+    )
+    stores[-1].start()
+
+    for store in stores:
+        store.wait()
     far_copy.wait_send()
     for stratum in range(2):
         for owner in range(groups):
@@ -400,7 +439,6 @@
     user_tiles, item_tiles, friend_tiles = users // edge, items // edge, friends // edge
     assert edge == rank and items == groups * edge and blocks > 2
     assert user_tiles % 2 == 0 and item_tiles % 2 == 0 and friend_tiles % 2 == 0
-    vmem = pl.BlockSpec(memory_space=pltpu.VMEM)
     hbm = pl.BlockSpec(memory_space=pltpu.HBM)
     dma = pltpu.SemaphoreType.DMA
     flops = 6 * rank * users * (2 * items + friends)
@@ -418,11 +456,12 @@
         functools.partial(strata_kernel, blocks, groups),
         out_shape=shapes,
         in_specs=[hbm] * 16,
-        out_specs=[vmem] * 6,
+        out_specs=[hbm] * 6,
         scratch_shapes=[
             pltpu.VMEM((users, rank), f32),
             pltpu.VMEM((users, edge), f32),
             pltpu.VMEM((users, rank), bf16),
+            pltpu.VMEM((rank, users), bf16),
             pltpu.VMEM((rank, users), bf16),
             pltpu.VMEM((friends, rank), f32),
             pltpu.VMEM((friends, rank), bf16),
@@ -459,12 +498,14 @@
             pltpu.VMEM((groups, edge, rank), bf16),
             pltpu.VMEM((groups, edge, rank), f32),
             pltpu.VMEM((groups, edge, rank), bf16),
+            pltpu.VMEM((edge, rank), f32),
+            pltpu.VMEM((1, edge), f32),
             pltpu.VMEM((edge, rank), bf16),
             pltpu.VMEM((edge + 8, rank), f32),
             pltpu.VMEM((edge + 8, rank), f32),
             pltpu.VMEM((friends, rank), bf16),
             pltpu.VMEM((friends, rank), bf16),
-            dma((18,)), dma,
+            dma((18,)), dma((5 + friend_tiles // 2,)), dma,
             dma, dma,
             dma((2, groups)), dma((2, groups)),
             dma((groups,)), dma((groups,)),

time: 34.5 us -> 33.3 us (0.965)
  Pallas kernels: 33 us -> 31.9 us
    pallas_call x1, Pallas kernels: 30.9 us -> 29.7 us  [local(): pl.pallas_call(functools.partial(strata_kernel, blocks, groups), out_shap...]
where the time goes in v3:
time: 33.3 us; the launch traced here: 33.2 us
  Pallas kernels  31.9 us (96%)
  between operations  1.29 us (4%)
    pallas_call x1, Pallas kernels, local(): pl.pallas_call(functools.partial(strata_kernel, blocks, groups), out_shap...  29.7 us
    pallas_call x1, Pallas kernels, local(): pl.pallas_call(functools.partial(finish_kernel, len(shapes)), out_shape=s...  2.13 us

profile of v3, /device:TPU:0, one launch (start us, length us, event | category | flops | bytes accessed | tf_op | source)
XLA Modules:
  0.0 33.2 jit_solution(15864680866864274259)
XLA Ops:
  1.3 29.7 %strata.1 = (f32[1024,128]{1,0:T(8,128)}, f32[8,128]{1,0:T(8,128)}, f32[1024,128]{1,0:T(8,128)}, f32[8,128]{1,0:T(8,128)}, f32[128,128]{1,0:T(8,128)}, /*index=5*/f32[1,128]{1,0:T(1,128)}) custom-call(f32[1024,128]{1,0:T(8,128)} %user_hbm.1, f32[1024,128]{1,0:T(8,128)} %friend_hbm.1, f32[512,128]{1,0:T(8,128)} %item_hbm.1, f32[8,128]{1,0:T(8,128)} %bitcast.15, ...), custom_call_target="tpu_custom_call" | custom-call | flops 1610612736 | bytes 8388608 | tf_op jit(solution)/shard_map/strata/pallas_call | solution.py:455
  31.0 2.1 %finish.1 = (f32[1024,128]{1,0:T(8,128)}, f32[8,128]{1,0:T(8,128)}, f32[1024,128]{1,0:T(8,128)}, f32[8,128]{1,0:T(8,128)}, f32[128,128]{1,0:T(8,128)}, /*index=5*/f32[1,128]{1,0:T(1,128)}) custom-call(f32[1024,128]{1,0:T(8,128)} %get-tuple-element.18.refs_0_, f32[8,128]{1,0:T(8,128)} %get-tuple-element.19.refs_1_, f32[1024,128]{1,0:T(8,128)} %get-tuple-element.20.refs_2_, ...), custom_call_target="tpu_custom_call" | custom-call | tf_op jit(solution)/shard_map/finish/pallas_call | solution.py:532

commit v4 on v3

--- a/solution.py
+++ b/solution.py
@@ -128,7 +128,7 @@
         device_id=(partner, g), device_id_type=MESH,
     )
 
-    for n in range(11):
+    for n in range(9):
         loads[n].wait()
     tables = [
         (
@@ -154,10 +154,11 @@
         user_low[rows, :] = state.astype(bf16)
         target_t[:, rows] = state.T.astype(bf16)
 
+    loads[9].wait()
+    loads[10].wait()
     for tile in range(user_tiles):
         rows = pl.ds(tile * edge, edge)
         keep_user(user_t, rows, user[rows, :])
-        user_acc[rows, :] = as_columns(user_accum[pl.ds(tile, 1), :], edge)
     item_low[...] = item[...].astype(bf16)
     table_copy.wait()
 
@@ -269,6 +270,8 @@
             pl.semaphore_wait(barrier, 2 * groups)
         send_parts(0, user_t, residual, chunk)
 
+    for tile in range(user_tiles):
+        user_acc[pl.ds(tile * edge, edge), :] = as_columns(user_accum[pl.ds(tile, 1), :], edge)
     loads[13].wait()
     friend_low[...] = friend[...].astype(bf16)
     far_copy.start()
@@ -409,14 +412,27 @@
         back_copy(chunk).wait_send()
 
 
-def finish_kernel(count, *refs):
+def result_pieces(shapes):
+    return [
+        (n, first, min(256, shape.shape[0] - first))
+        for n, shape in enumerate(shapes)
+        for first in range(0, shape.shape[0], 256)
+    ]
+
+
+def finish_kernel(pieces, count, *refs):
     sources, targets, held = refs[:count], refs[count : 2 * count], refs[2 * count : -2]
-    fills = [
-        pltpu.make_async_copy(sources[n], held[n], refs[-2].at[n]) for n in range(count)
-    ]
-    drains = [
-        pltpu.make_async_copy(held[n], targets[n], refs[-1].at[n]) for n in range(count)
-    ]
+
+    def copies(froms, tos, sems):
+        return [
+            pltpu.make_async_copy(
+                froms[n].at[pl.ds(first, rows), :], tos[n].at[pl.ds(first, rows), :], sems.at[m]
+            )
+            for m, (n, first, rows) in enumerate(pieces)
+        ]
+
+    fills = copies(sources, held, refs[-2])
+    drains = copies(held, targets, refs[-1])
     for copy in fills:
         copy.start()
     for fill, drain in zip(fills, drains):
@@ -450,6 +466,7 @@
         jax.ShapeDtypeStruct((edge, rank), f32),
         jax.ShapeDtypeStruct((1, edge), f32),
     ]
+    pieces = result_pieces(shapes)
     rate_slots, mask_words = rating_masks.shape[1:3]
     trust_slots = trust_masks.shape[0]
     results = pl.pallas_call(
@@ -530,12 +547,12 @@
         trust_values, trust_masks.transpose(1, 0, 2),
     )
     results = pl.pallas_call(
-        functools.partial(finish_kernel, len(shapes)),
+        functools.partial(finish_kernel, pieces, len(shapes)),
         out_shape=shapes,
         in_specs=[hbm] * len(shapes),
         out_specs=[hbm] * len(shapes),
         scratch_shapes=[pltpu.VMEM(shape.shape, shape.dtype) for shape in shapes]
-        + [dma((len(shapes),)), dma((len(shapes),))],
+        + [dma((len(pieces),)), dma((len(pieces),))],
         compiler_params=pltpu.CompilerParams(vmem_limit_bytes=58 * 1024 * 1024),
         name="finish",
     )(*results)

time: 33.3 us -> 33.4 us (level)
  no operation moved by 1% of the time
where the time goes in v4:
time: 33.4 us; the launch traced here: 33.2 us
  Pallas kernels  31.9 us (96%)
  between operations  1.29 us (4%)
    pallas_call x1, Pallas kernels, local(): pl.pallas_call(functools.partial(strata_kernel, blocks, groups), out_shap...  29.7 us
    pallas_call x1, Pallas kernels, local(): pl.pallas_call(functools.partial(finish_kernel, pieces, len(shapes)), out...  2.19 us

profile of v4, /device:TPU:0, one launch (start us, length us, event | category | flops | bytes accessed | tf_op | source)
XLA Modules:
  0.0 33.2 jit_solution(2040943328825599626)
XLA Ops:
  1.3 29.7 %strata.1 = (f32[1024,128]{1,0:T(8,128)}, f32[8,128]{1,0:T(8,128)}, f32[1024,128]{1,0:T(8,128)}, f32[8,128]{1,0:T(8,128)}, f32[128,128]{1,0:T(8,128)}, /*index=5*/f32[1,128]{1,0:T(1,128)}) custom-call(f32[1024,128]{1,0:T(8,128)} %user_hbm.1, f32[1024,128]{1,0:T(8,128)} %friend_hbm.1, f32[512,128]{1,0:T(8,128)} %item_hbm.1, f32[8,128]{1,0:T(8,128)} %bitcast.15, ...), custom_call_target="tpu_custom_call" | custom-call | flops 1610612736 | bytes 8388608 | tf_op jit(solution)/shard_map/strata/pallas_call | solution.py:472
  31.0 2.2 %finish.1 = (f32[1024,128]{1,0:T(8,128)}, f32[8,128]{1,0:T(8,128)}, f32[1024,128]{1,0:T(8,128)}, f32[8,128]{1,0:T(8,128)}, f32[128,128]{1,0:T(8,128)}, /*index=5*/f32[1,128]{1,0:T(1,128)}) custom-call(f32[1024,128]{1,0:T(8,128)} %get-tuple-element.18.refs_0_, f32[8,128]{1,0:T(8,128)} %get-tuple-element.19.refs_1_, f32[1024,128]{1,0:T(8,128)} %get-tuple-element.20.refs_2_, ...), custom_call_target="tpu_custom_call" | custom-call | tf_op jit(solution)/shard_map/finish/pallas_call | solution.py:549
